TPU v7x, 512 devices: a whole 4x8x8 slice. The times are simulated.
512 devices in a mesh: ctx: 64 (over x, z, core), head: 8 (over y).
Axes of the slice: x: 4, y: 8, z: 8, core: 2. Of those that a mesh axis runs over, the one named last changes fastest.
Arguments:
- qkv: bfloat16 [1, 65536, 6144], P(None, ('ctx', 'head')), may hold values from -6 to 6
- grad_out: bfloat16 [1, 65536, 2048], P(None, ('ctx', 'head')), may hold values from -6 to 6
- w_qkv: bfloat16 [2048, 6144], P('ctx', 'head'), may hold values from -0.078125 to 0.078125
Outputs:
- grad_input: float32 [1, 65536, 2048], P(None, ('ctx', 'head'))
All inputs are finite; a program needn't handle non-finite values.
Results may differ from a plain program's by a relative error of at most 0.02.
Values may be sent and summed in bfloat16 or wider, within the bound.
A program may use at most 128 MiB of HBM per device.

v0:
```python
import math

import jax
import jax.numpy as jnp
from jax import lax
from jax.sharding import PartitionSpec as P

DH = 128


def carried_in(x, axis, join, neutral, backward):
    count = lax.axis_size(axis)
    place = lax.axis_index(axis)
    ahead = count - 1 - place if backward else place
    gathered = lax.all_gather(x.astype(jnp.bfloat16), axis)
    state = jnp.zeros_like(x) + jnp.asarray(neutral, x.dtype)

    def one(step, state):
        source = count - 1 - step if backward else step
        return join(state, lax.dynamic_index_in_dim(gathered, source, 0, False).astype(x.dtype))

    return lax.fori_loop(0, ahead, one, state)


def combine_sum(earlier, later):
    return earlier + later


def per_device(qkv, grad_out, w_qkv):
    highest = lax.Precision.HIGHEST
    whole_weight = lax.all_gather(w_qkv, "ctx", axis=0, tiled=True)
    local_qkv, local_grad = (
        lax.all_to_all(qkv, "head", split_axis=2, concat_axis=1, tiled=True),
        lax.all_to_all(grad_out, "head", split_axis=2, concat_axis=1, tiled=True),
    )
    num_seqs, block_len, width3 = local_qkv.shape
    heads_here = width3 // (3 * DH)
    factor = 1.0 / math.sqrt(DH * block_len * lax.axis_size("ctx"))
    blocks = local_qkv.reshape(num_seqs, block_len, heads_here, 3, DH)
    query_rows = blocks[:, :, :, 0]
    key_rows = blocks[:, :, :, 1]
    value_rows = blocks[:, :, :, 2]
    grad_rows = local_grad.reshape(num_seqs, block_len, heads_here, DH)
    kv_own = jnp.einsum("sthd,sthe->shde", key_rows, value_rows, preferred_element_type=jnp.float32)
    qg_own = jnp.einsum(
        "sthd,sthe->shde", query_rows, grad_rows, preferred_element_type=jnp.float32
    )
    empty_state = jnp.zeros_like(kv_own)
    kv_before = carried_in(kv_own, "ctx", combine_sum, empty_state, False)
    qg_after = carried_in(qg_own, "ctx", combine_sum, empty_state, True)
    positions = lax.broadcasted_iota(jnp.int32, (block_len, block_len), 0)
    columns = lax.broadcasted_iota(jnp.int32, (block_len, block_len), 1)
    causal = (positions >= columns).astype(jnp.float32)
    scores_gv = (
        jnp.einsum("sthe,suhe->shtu", grad_rows, value_rows, preferred_element_type=jnp.float32)
        * causal
    )
    scores_qk = (
        jnp.einsum("sthd,suhd->shtu", query_rows, key_rows, preferred_element_type=jnp.float32)
        * causal
    )
    key_wide = key_rows.astype(jnp.float32)
    grad_wide = grad_rows.astype(jnp.float32)
    grad_q = jnp.einsum("shtu,suhd->sthd", scores_gv, key_wide, precision=highest) + jnp.einsum(
        "sthe,shde->sthd", grad_wide, kv_before, precision=highest
    )
    query_wide = query_rows.astype(jnp.float32)
    value_wide = value_rows.astype(jnp.float32)
    grad_k = jnp.einsum("shtu,sthd->suhd", scores_gv, query_wide, precision=highest) + jnp.einsum(
        "suhe,shde->suhd", value_wide, qg_after, precision=highest
    )
    grad_v = jnp.einsum("shtu,sthe->suhe", scores_qk, grad_wide, precision=highest) + jnp.einsum(
        "suhd,shde->suhe", key_wide, qg_after, precision=highest
    )
    gradients = (
        (jnp.stack([grad_q, grad_k, grad_v], axis=3) * factor)
        .astype(jnp.bfloat16)
        .reshape(num_seqs, block_len, width3)
    )
    own_rows = lax.psum_scatter(
        jnp.einsum(
            "stf,df->tsd", gradients, whole_weight, preferred_element_type=jnp.float32
        ).astype(jnp.bfloat16),
        "head",
        scatter_dimension=0,
        tiled=True,
    ).astype(jnp.float32)
    return jnp.transpose(own_rows, (1, 0, 2))


def solution(mesh):
    in_specs = (P(None, ("ctx", "head"), None), P(None, ("ctx", "head"), None), P("ctx", "head"))
    out_specs = P(None, ("ctx", "head"), None)
    return jax.shard_map(
        per_device, mesh=mesh, in_specs=in_specs, out_specs=out_specs, check_vma=False
    )
```

profile of v0, /device:TPU:1, one launch (start us, length us, event | category | flops | bytes accessed | tf_op | source)
XLA Modules:
  0.0 456.7 jit_solution(5175588874633387678)
XLA Ops:
  6.5 2.3 copy.42
  9.4 11.4 %reduce = bf16[2048,128]{1,0:T(8,128)(2,1)S(1)} reduce(bf16[2048,1,128]{2,1,0:T(2,128)(2,1)S(1)} %bitcast.109, bf16[]{:T(256)} %broadcast.9), dimensions={1}, to_apply=%bitcast.91.reduce_sub_computation | reduce | bytes 1048578
  21.8 7.7 %all-to-all-start = ((bf16[8,2,16384]{2,1,0:T(2,128)(2,1)}), bf16[8,2,16384]{2,1,0:T(2,128)(2,1)}, u32[]{:S(2)}, u32[]{:S(2)}) async-start(bf16[8,2,16384]{2,1,0:T(2,128)(2,1)} %reshape.156), calls=%async_computation | async-start | bytes 1048576 | tf_op jit(solution)/shard_map/all_to_all | solution.py:34
  29.4 6.8 %copy.44 = bf16[1,128,6144]{1,0,2:T(2,128)(2,1)S(1)} copy(bf16[1,128,6144]{2,1,0:T(8,128)(2,1)} %param.7) | data formatting | bytes 3145728 | tf_op args[0]
  36.2 34.3 %reduce.1 = bf16[6144,128]{1,0:T(8,128)(2,1)} reduce(bf16[6144,1,128]{2,1,0:T(2,128)(2,1)S(1)} %bitcast.105, bf16[]{:T(256)} %broadcast.9), dimensions={1}, to_apply=%bitcast.93.reduce_sub_computation | reduce | bytes 3145730
  70.6 3.7 reshape.158
  74.3 6.6 %all-to-all-start.1 = ((bf16[8,2,49152]{2,1,0:T(2,128)(2,1)}), bf16[8,2,49152]{2,1,0:T(2,128)(2,1)}, u32[]{:S(2)}, u32[]{:S(2)}) async-start(bf16[8,2,49152]{2,1,0:T(2,128)(2,1)} %reshape.158), calls=%async_computation.1 | async-start | bytes 3145728 | tf_op jit(solution)/shard_map/all_to_all | solution.py:33
  81.2 2.2 reshape.157
  84.8 33.7 %all-to-all-done.1 = bf16[8,2,49152]{2,1,0:T(2,128)(2,1)} async-done(((bf16[8,2,49152]{2,1,0:T(2,128)(2,1)}), bf16[8,2,49152]{2,1,0:T(2,128)(2,1)}, u32[]{:S(2)}, u32[]{:S(2)}) %all-to-all-start.1) | async-done | bytes 1572896 | tf_op jit(solution)/shard_map/all_to_all | solution.py:33
  118.5 4.7 %reshape.159 = bf16[6144,1,128]{2,1,0:T(2,128)(2,1)S(1)} reshape(bf16[8,2,49152]{2,1,0:T(2,128)(2,1)} %all-to-all-done.1) | data formatting | bytes 3145728
  123.4 2.2 copy.45
  125.6 2.5 reshape.145
  131.4 4.5 fusion.24
  137.2 4.3 fusion.14
  141.5 5.0 %fusion.11 = f32[2,128,1024]{2,1,0:T(8,128)S(1)} fusion(f32[2,1024,1024]{2,1,0:T(8,128)S(1)} %fusion.23, f32[1024,1024]{1,0:T(8,128)S(1)} %fusion.9, bf16[1,1024,2,3,128]{1,4,3,2,0:T(8,128)(2,1)S(1)} %reshape.145), kind=kOutput, calls=%fused_computation.16 | convolution fusion | flops 3223322624 | bytes 14155776 | tf_op jit(solution)/shard_map/shtu,suhd->sthd/dot_general | solution.py:64
  146.6 8.0 %fusion.17 = f32[2,128,1024]{2,1,0:T(8,128)} fusion(bf16[1024,2,128]{0,2,1:T(8,128)(2,1)S(1)} %copy-done, f32[2,1024,1024]{2,1,0:T(8,128)} %fusion.24, f32[1024,1024]{1,0:T(8,128)S(1)} %fusion.9), kind=kOutput, calls=%fused_computation.18 | convolution fusion | flops 3223322624 | bytes 14155776 | tf_op jit(solution)/shard_map/shtu,sthe->suhe/dot_general | solution.py:72
  154.6 62.5 %all-gather.10.cloned.1.call-done = bf16[128,128,128]{2,1,0:T(8,128)(2,1)} async-done(((bf16[2,128,128]{2,1,0:T(8,128)(2,1)}), bf16[128,128,128]{2,1,0:T(8,128)(2,1)}) %all-gather.10.cloned.1.call-update) | async-done | bytes 4194320 | tf_op jit(solution)/shard_map/all_gather | solution.py:15
  217.1 55.0 %while.23 = (s32[]{:T(128)}, f32[1,2,128,128]{3,2,1,0:T(8,128)S(1)}, s32[]{:T(128)}, bf16[64,1,2,128,128]{4,3,2,1,0:T(8,128)(2,1)}, s32[]{:T(128)}, /*index=5*/s32[]{:T(128)}, s32[]{:T(128)}, s32[]{:T(128)}) while((s32[]{:T(128)}, f32[1,2,128,128]{3,2,1,0:T(8,128)S(1)}, s32[]{:T(128)}, bf16[64,1,2,128,128]{4,3,2,1,0:T(8,128)(2,1)}, s32[]{:T(128)}, ...), condition=%wide.region_3.4_spmd, body=%wide.region_2.3_spmd.sunk | while | flops 65542 | bytes 327823 | solution.py:22
  272.1 2.9 fusion.20
  276.6 25.6 %all-gather.8.cloned.1.call-done = bf16[128,128,128]{2,1,0:T(8,128)(2,1)} async-done(((bf16[2,128,128]{2,1,0:T(8,128)(2,1)}), bf16[128,128,128]{2,1,0:T(8,128)(2,1)}) %all-gather.8.cloned.1.call-update) | async-done | bytes 4194320 | tf_op jit(solution)/shard_map/all_gather | solution.py:15
  304.9 81.9 %all-gather.6.cloned.1.call-done = bf16[2048,768]{1,0:T(8,128)(2,1)} async-done(((bf16[32,768]{1,0:T(8,128)(2,1)}), bf16[2048,768]{1,0:T(8,128)(2,1)}) %all-gather.6.cloned.1.call-update) | async-done | bytes 3145744 | tf_op jit(solution)/shard_map/all_gather | solution.py:31
  386.8 6.9 %convert_bitcast_fusion = bf16[1024,1,2048]{2,0,1:T(8,128)(2,1)} fusion(bf16[1024,768]{0,1:T(8,128)(2,1)S(1)} %bitcast.111, bf16[2048,768]{1,0:T(8,128)(2,1)} %all-gather.6.cloned.1.call-done), kind=kOutput, calls=%fused_computation.8 | convolution fusion | flops 3223322624 | bytes 8912896 | tf_op jit(solution)/shard_map/stf,df->tsd/dot_general | solution.py:81
  393.8 54.2 %reduce-scatter.2.cloned.1.call-done = bf16[128,1,2048]{2,0,1:T(8,128)(2,1)} async-done(((bf16[1024,1,2048]{2,0,1:T(8,128)(2,1)}), bf16[128,1,2048]{2,0,1:T(8,128)(2,1)}) %reduce-scatter.2.cloned.1.call-update) | async-done | bytes 524304 | tf_op jit(solution)/shard_map/reduce_scatter | solution.py:80
  448.0 2.1 bitcast_convert_fusion
  (97 shorter events, 66.5 us)
Async XLA Ops:
  21.8 52.5 %all-to-all-start = ((bf16[8,2,16384]{2,1,0:T(2,128)(2,1)}), bf16[8,2,16384]{2,1,0:T(2,128)(2,1)}, u32[]{:S(2)}, u32[]{:S(2)}) async-start(bf16[8,2,16384]{2,1,0:T(2,128)(2,1)} %reshape.156), calls=%async_computation | async-start | bytes 1048576 | tf_op jit(solution)/shard_map/all_to_all | solution.py:34
  74.3 44.2 %all-to-all-start.1 = ((bf16[8,2,49152]{2,1,0:T(2,128)(2,1)}), bf16[8,2,49152]{2,1,0:T(2,128)(2,1)}, u32[]{:S(2)}, u32[]{:S(2)}) async-start(bf16[8,2,49152]{2,1,0:T(2,128)(2,1)} %reshape.158), calls=%async_computation.1 | async-start | bytes 3145728 | tf_op jit(solution)/shard_map/all_to_all | solution.py:33
  80.9 136.1 %all-gather.10.cloned.1.call-start = ((), (), s32[]{:S(2)}) async-start(), calls=%async_computation.6 | async-start | bytes 4259840 | tf_op jit(solution)/shard_map/all_gather | solution.py:15
  123.4 4.7 %copy-start = (bf16[1024,2,128]{0,2,1:T(8,128)(2,1)S(1)}, bf16[1024,2,128]{0,2,1:T(8,128)(2,1)}, u32[]{:S(2)}) copy-start(bf16[1024,2,128]{0,2,1:T(8,128)(2,1)} %reshape.144) | copy-start | bytes 1572868
  129.1 173.1 %all-gather.8.cloned.1.call-start = ((), (), s32[]{:S(2)}) async-start(), calls=%async_computation.5 | async-start | bytes 4259840 | tf_op jit(solution)/shard_map/all_gather | solution.py:15
  130.1 256.7 %all-gather.6.cloned.1.call-start = ((), (), s32[]{:S(2)}) async-start(), calls=%async_computation.3 | async-start | bytes 3194880 | tf_op jit(solution)/shard_map/all_gather | solution.py:31
  130.8 317.2 %reduce-scatter.2.cloned.1.call-start = ((), (), s32[]{:S(2)}) async-start(), calls=%async_computation.4 | async-start | bytes 4718592 | tf_op jit(solution)/shard_map/reduce_scatter | solution.py:80
  272.1 2.9 copy-start.1
  276.6 27.2 %copy-start.2 = (f32[1,1024,2,1,128]{1,4,2,3,0:T(8,128)S(1)}, f32[1,1024,2,1,128]{1,4,2,3,0:T(8,128)}, u32[]{:S(2)}) copy-start(f32[1,1024,2,1,128]{1,4,2,3,0:T(8,128)} %fusion.20) | copy-start | bytes 3145732
  303.1 1.2 copy-start.3
Sparse Core Ops, SparseCore 0:
  129.2 87.7 all-gather.9
  220.4 81.7 all-gather.7
  305.6 81.2 all-gather.5
  393.9 54.0 reduce-scatter.1
where the time goes:
time: 460 us; the launch traced here: 457 us
  waiting for transfers between devices  259 us (56%)
  other arithmetic  103 us (22%)
  matrix products  37.1 us (8%)
  local copies, waits for them, and re-layouts  28.3 us (6%)
  starting transfers between devices  14.6 us (3%)
  between operations  13.3 us (3%)
    all_gather x2, waiting for transfers between devices, carried_in(): gathered = lax.all_gather(x.astype(jnp.bfloat16), axis)  88.1 us
    all_gather x1, waiting for transfers between devices, per_device(): whole_weight = lax.all_gather(w_qkv, 'ctx', axis=0, tiled=True)  81.9 us
    add x63, other arithmetic, combine_sum(): return earlier + later  54.4 us
    reduce_scatter x1, waiting for transfers between devices, per_device(): lax.psum_scatter(jnp.einsum('stf,df->tsd', gradients, whole_weight, prefe...  54.2 us
    unnamed x2, other arithmetic  45.8 us
    all_to_all x1, waiting for transfers between devices, per_device(): lax.all_to_all(qkv, 'head', split_axis=2, concat_axis=1, tiled=True)  33.7 us
    unnamed x17, local copies, waits for them, and re-layouts  22.1 us
  transfers between devices with their start and end apart: 6, of which 5 were waited for; matrix products, arithmetic and copies ran while one was open for 29% of the time, Pallas kernels for 0%

commit v1 on v0

v1 whole, which is shorter than its diff:
```python
import functools
import math

import jax
import jax.numpy as jnp
from jax import lax
from jax.experimental import pallas as pl
from jax.experimental.pallas import tpu as pltpu
from jax.sharding import PartitionSpec as P

DH = 128
W3 = 3 * DH
MESH = pl.DeviceIdType.MESH
NX, NY, NZ = 4, 8, 8
F32, BF16 = jnp.float32, jnp.bfloat16


def where_am_i():
    ctx, y = lax.axis_index("ctx"), lax.axis_index("head")
    c, xz = lax.rem(ctx, 2), lax.div(ctx, 2)
    return lax.div(xz, NZ), y, lax.rem(xz, NZ), c


def device(x, y, z, c):
    return ((x * NZ + z) * 2 + c, y)


def nn(a, b):
    return lax.dot_general(a, b, (((1,), (0,)), ((), ())), preferred_element_type=F32)


def nt(a, b):
    return lax.dot_general(a, b, (((1,), (1,)), ((), ())), preferred_element_type=F32)


def tn(a, b):
    return lax.dot_general(a, b, (((0,), (0,)), ((), ())), preferred_element_type=F32)


def lanes(index, width):
    return pl.ds(pl.multiple_of(index * width, width), width)


def attention_kernel(
    factor, qkv_ref, grad_ref, out_ref,
    got_qkv, got_grad, states, arrived, before, intra, total, z_in, x_in, z_out, base,
    core_sem, state_send, state_recv, z_send, z_recv, x_send, x_recv, b_send, b_recv, p_send, p_recv,
):
    x, y, z, c = where_am_i()
    other = 1 - c
    ring_y = lambda k: device(x, lax.rem(y + k, NY), z, c)
    ring_z = lambda k: device(x, y, lax.rem(z + k, NZ), c)
    ring_x = lambda k: device(lax.rem(x + k, NX), y, z, c)
    partner = device(x, y, z, other)

    barrier = pltpu.get_barrier_semaphore()
    everyone = [partner] + [ring_y(k) for k in range(1, NY)]
    everyone += [ring_z(k) for k in range(1, NZ)] + [ring_x(k) for k in range(1, NX)]
    for peer in everyone:
        pl.semaphore_signal(barrier, inc=1, device_id=peer, device_id_type=MESH)
    pl.semaphore_wait(barrier, len(everyone))

    def swap(j):
        send = pltpu.make_async_remote_copy(
            qkv_ref.at[:, lanes(2 * j + other, W3)], got_qkv.at[:, lanes(j, W3)],
            core_sem.at[0, j], core_sem.at[1, j], device_id=partner, device_id_type=MESH)
        send_grad = pltpu.make_async_remote_copy(
            grad_ref.at[:, lanes(2 * j + other, DH)], got_grad.at[:, lanes(j, DH)],
            core_sem.at[2, j], core_sem.at[3, j], device_id=partner, device_id_type=MESH)
        return send, send_grad

    def y_of(k):
        return lax.rem(y + k, NY)

    def start_swap(k, carry):
        for copy in swap(y_of(k)):
            copy.start()
        return carry

    lax.fori_loop(0, NY, start_swap, 0)

    def own_rows(j):
        at = (2 * j + c) * W3
        part = lambda i: qkv_ref[:, pl.ds(pl.multiple_of(at + i * DH, DH), DH)]
        return part(0), part(1), part(2), grad_ref[:, lanes(2 * j + c, DH)]

    def got_rows(j):
        part = lambda i: got_qkv[:, pl.ds(pl.multiple_of(j * W3 + i * DH, DH), DH)]
        return part(0), part(1), part(2), got_grad[:, lanes(j, DH)]

    def state_copy(k):
        return pltpu.make_async_remote_copy(
            states.at[y_of(k)], arrived.at[y], state_send.at[k], state_recv.at[k],
            device_id=ring_y(k), device_id_type=MESH)

    def block_states(into, j):
        for slot, rows in ((c, own_rows(j)), (other, got_rows(j))):
            q, k, v, g = rows
            into[j, slot, 0] = tn(k, v).astype(BF16)
            into[j, slot, 1] = tn(q, g).astype(BF16)

    def make_states(k, carry):
        j = y_of(k)
        for copy in swap(j):
            copy.wait()
        block_states(states, j)
        state_copy(k).start()
        return carry

    lax.fori_loop(1, NY, make_states, 0)
    for copy in swap(y):
        copy.wait()
    block_states(arrived, y)

    rows_at = lax.broadcasted_iota(jnp.int32, (DH, DH), 0)
    cols_at = lax.broadcasted_iota(jnp.int32, (DH, DH), 1)
    causal = rows_at >= cols_at

    def inside(j, carry):
        for slot, rows in ((c, own_rows(j)), (other, got_rows(j))):
            q, k, v, g = rows
            gv = jnp.where(causal, nt(g, v), 0.0).astype(BF16)
            qk = jnp.where(causal, nt(q, k), 0.0).astype(BF16)
            intra[slot, j, 0] = nn(gv, k)
            intra[slot, j, 1] = tn(gv, q)
            intra[slot, j, 2] = tn(qk, g)
        return carry

    lax.fori_loop(0, NY, inside, 0)

    def wait_state(k, carry):
        state_copy(k).wait()
        return carry

    lax.fori_loop(1, NY, wait_state, 0)

    for kind in range(2):
        acc = jnp.zeros((DH, DH), F32)
        for j in range(NY):
            acc = acc + arrived[j, 0, kind].astype(F32) + arrived[j, 1, kind].astype(F32)
        total[pl.ds(kind * DH, DH), :] = acc
    part = 2 * DH // NZ

    def slice_of(i):
        return pl.ds(pl.multiple_of(i * part, part), part)

    def z_copy(k):
        return pltpu.make_async_remote_copy(
            total.at[slice_of(lax.rem(z + k, NZ))], z_in.at[z], z_send.at[k], z_recv.at[k],
            device_id=ring_z(k), device_id_type=MESH)

    for k in range(1, NZ):
        z_copy(k).start()
    z_in[z] = total[slice_of(z), :]
    for k in range(1, NZ):
        z_copy(k).wait()
    sums = [jnp.zeros((part, DH), F32)]
    for i in range(NZ):
        sums.append(sums[-1] + z_in[i])
    x_in[x] = sums[NZ]

    def x_copy(k):
        return pltpu.make_async_remote_copy(
            x_in.at[x], x_in.at[x], x_send.at[k], x_recv.at[k],
            device_id=ring_x(k), device_id_type=MESH)

    for k in range(1, NX):
        x_copy(k).start()
    forward = z < NZ // 2
    for k in range(1, NX):
        x_copy(k).wait()
    far = jnp.zeros((part, DH), F32)
    for i in range(NX):
        counts = jnp.where(forward, i < x, i > x)
        far = far + jnp.where(counts, x_in[i], 0.0)
    for i in range(NZ):
        near = jnp.where(forward, sums[i], sums[NZ] - sums[i + 1])
        z_out[i] = far + near

    def b_copy(k):
        return pltpu.make_async_remote_copy(
            z_out.at[lax.rem(z + k, NZ)], base.at[slice_of(z)], b_send.at[k], b_recv.at[k],
            device_id=ring_z(k), device_id_type=MESH)

    for k in range(1, NZ):
        b_copy(k).start()
    base[slice_of(z), :] = z_out[z]
    for k in range(1, NZ):
        b_copy(k).wait()

    acc = base[pl.ds(0, DH), :]
    for slot in range(2):
        for j in range(NY):
            states[j, slot, 0] = acc.astype(BF16)
            acc = acc + arrived[j, slot, 0].astype(F32)
    acc = base[pl.ds(DH, DH), :]
    for slot in (1, 0):
        for j in reversed(range(NY)):
            states[j, slot, 1] = acc.astype(BF16)
            acc = acc + arrived[j, slot, 1].astype(F32)

    def p_copy(k):
        return pltpu.make_async_remote_copy(
            states.at[y_of(k)], before.at[y], p_send.at[k], p_recv.at[k],
            device_id=ring_y(k), device_id_type=MESH)

    def start_p(k, carry):
        p_copy(k).start()
        return carry

    lax.fori_loop(1, NY, start_p, 0)
    for slot in range(2):
        for kind in range(2):
            before[y, slot, kind] = states[y, slot, kind]

    def finish(j):
        for slot, rows in ((c, own_rows(j)), (other, got_rows(j))):
            q, k, v, g = rows
            kv, qg = before[j, slot, 0], before[j, slot, 1]
            at = lambda i: pl.ds(pl.multiple_of(j * W3 + i * DH, DH), DH)
            out_ref[slot, :, at(0)] = ((intra[slot, j, 0] + nt(g, kv)) * factor).astype(BF16)
            out_ref[slot, :, at(1)] = ((intra[slot, j, 1] + nt(v, qg)) * factor).astype(BF16)
            out_ref[slot, :, at(2)] = ((intra[slot, j, 2] + nn(k, qg)) * factor).astype(BF16)

    finish(y)

    def finish_got(k, carry):
        p_copy(k).wait()
        finish(lax.rem(y - k + NY, NY))
        return carry

    lax.fori_loop(1, NY, finish_got, 0)


def attention(qkv, grad, factor):
    state = pltpu.VMEM((NY, 2, 2, DH, DH), BF16)
    part = 2 * DH // NZ
    pairs = [pltpu.SemaphoreType.DMA((n,)) for n in (NY, NY, NZ, NZ, NX, NX, NZ, NZ, NY, NY)]
    return pl.pallas_call(
        functools.partial(attention_kernel, factor),
        out_shape=jax.ShapeDtypeStruct((2, DH, NY * W3), BF16),
        in_specs=[pl.BlockSpec(memory_space=pltpu.VMEM)] * 2,
        out_specs=pl.BlockSpec(memory_space=pltpu.VMEM),
        scratch_shapes=[
            pltpu.VMEM((DH, NY * W3), BF16), pltpu.VMEM((DH, NY * DH), BF16),
            state, state, state,
            pltpu.VMEM((2, NY, 3, DH, DH), F32),
            pltpu.VMEM((2 * DH, DH), F32), pltpu.VMEM((NZ, part, DH), F32),
            pltpu.VMEM((NX, part, DH), F32), pltpu.VMEM((NZ, part, DH), F32),
            pltpu.VMEM((2 * DH, DH), F32),
            pltpu.SemaphoreType.DMA((4, NY)), *pairs,
        ],
        compiler_params=pltpu.CompilerParams(
            collective_id=0, has_side_effects=True, vmem_limit_bytes=24 << 20),
        cost_estimate=pl.CostEstimate(flops=2 * 10**9, bytes_accessed=200 * 10**6, transcendentals=0),
        name="attention",
    )(qkv, grad)


def per_device(qkv, grad_out, w_qkv):
    n = lax.axis_size("ctx")
    factor = 1.0 / math.sqrt(DH * DH * NY * n)
    c = lax.rem(lax.axis_index("ctx"), 2)
    halves = jnp.stack([w_qkv[:, :W3], w_qkv[:, W3:]])
    keep = lax.dynamic_index_in_dim(halves, c, 0, False)
    give = lax.dynamic_index_in_dim(halves, 1 - c, 0, False)
    got = lax.ppermute(give, "ctx", [(i, i ^ 1) for i in range(n)])
    pair = jnp.where(c == 0, jnp.stack([keep, got]), jnp.stack([got, keep]))
    groups = [[2 * i + core for i in range(n // 2)] for core in range(2)]
    by_head = lax.all_gather(pair, "head")
    whole = lax.all_gather(by_head, "ctx", axis_index_groups=groups)
    grads = attention(qkv[0], grad_out[0], factor)
    grads = grads.reshape(2, DH, NY, W3)
    partial = jnp.einsum("btyf,xyprf->btxpr", grads, whole, preferred_element_type=F32)
    partial = partial.reshape(2, DH, -1)
    mine = lax.dynamic_index_in_dim(partial, c, 0, False)
    theirs = lax.dynamic_index_in_dim(partial, 1 - c, 0, False).astype(BF16)
    other = lax.ppermute(theirs, "ctx", [(i, i ^ 1) for i in range(n)])
    return (mine + other.astype(F32))[None]


def solution(mesh):
    spec = P(None, ("ctx", "head"), None)
    return jax.shard_map(
        per_device, mesh=mesh, in_specs=(spec, spec, P("ctx", "head")), out_specs=spec, check_vma=False)
```

time: 460 us -> 201 us (0.44)
  waiting for transfers between devices: 259 us -> 51.3 us
  other arithmetic: 103 us -> 1.13 us
  Pallas kernels: 0 us -> 80.8 us
  matrix products: 37.1 us -> 6.45 us
  blocking collectives: 0 us -> 21.2 us
  local copies, waits for them, and re-layouts: 28.3 us -> 14.9 us
    all_gather x3 -> x1, waiting for transfers between devices: 170 us -> 49 us  [per_device(): whole = lax.all_gather(by_head, 'ctx', axis_index_groups=groups)]
    pallas_call x0 -> x1, Pallas kernels: none -> 80.8 us  [attention(): pl.pallas_call(functools.partial(attention_kernel, factor), out_shape=jax...]
    add x63 -> x0, other arithmetic: 54.4 us -> none  [combine_sum(): return earlier + later]
    reduce_scatter x1 -> x0, waiting for transfers between devices: 54.2 us -> none  [per_device(): lax.psum_scatter(jnp.einsum('stf,df->tsd', gradients, whole_weight, prefe...]
    unnamed x2 -> x0, other arithmetic: 45.8 us -> none
    all_to_all x2 -> x0, waiting for transfers between devices: 33.7 us -> none  [the longest x1 33.7 us: per_device(): lax.all_to_all(qkv, 'head', split_axis=2, concat_axis=1, tiled=True)]
    dot_general x11 -> x1, matrix products: 37.1 us -> 6.45 us  [per_device(): jnp.einsum('btyf,xyprf->btxpr', grads, whole, preferred_element_type=F32)]
    all_gather x0 -> x1, blocking collectives: none -> 21.2 us  [per_device(): by_head = lax.all_gather(pair, 'head')]
  transfers between devices with their start and end apart: 6 -> 3, of which waited for: 5 -> 3; matrix products, arithmetic and copies ran while one was open for 29% -> 0% of each run, Pallas kernels for 0% -> 40%
where the time goes in v1:
time: 201 us
  Pallas kernels  80.8 us (40%)
  waiting for transfers between devices  51.3 us (26%)
  blocking collectives  21.2 us (11%)
  local copies, waits for them, and re-layouts  14.9 us (7%)
  between operations  13.5 us (7%)
  starting transfers between devices  11.7 us (6%)
  matrix products  6.45 us (3%)
    pallas_call x1, Pallas kernels, attention(): pl.pallas_call(functools.partial(attention_kernel, factor), out_shape=jax...  80.8 us
    all_gather x1, waiting for transfers between devices, per_device(): whole = lax.all_gather(by_head, 'ctx', axis_index_groups=groups)  49 us
    all_gather x1, blocking collectives, per_device(): by_head = lax.all_gather(pair, 'head')  21.2 us
    dot_general x1, local copies, waits for them, and re-layouts, per_device(): jnp.einsum('btyf,xyprf->btxpr', grads, whole, preferred_element_type=F32)  11.6 us
    ppermute x1, starting transfers between devices, per_device(): got = lax.ppermute(give, 'ctx', [(i, i ^ 1) for i in range(n)])  8.79 us
    dot_general x1, matrix products, per_device(): jnp.einsum('btyf,xyprf->btxpr', grads, whole, preferred_element_type=F32)  6.45 us
  transfers between devices with their start and end apart: 3, of which 3 were waited for; matrix products, arithmetic and copies ran while one was open for 0% of the time, Pallas kernels for 40%

profile of v1, /device:TPU:1, one launch (start us, length us, event | category | flops | bytes accessed | tf_op | source)
XLA Modules:
  0.0 201.0 jit_solution(2439736050497656384)
XLA Ops:
  6.5 0.0 all-gather.3.cloned.1.call-start
  6.5 0.8 slice_bitcast_fusion
  7.3 8.8 %collective-permute-start = (bf16[32,384]{1,0:T(8,128)(2,1)S(1)}, bf16[32,384]{1,0:T(8,128)(2,1)S(1)}, u32[]{:S(2)}, u32[]{:S(2)}) collective-permute-start(bf16[32,384]{1,0:T(8,128)(2,1)S(1)} %get-tuple-element.6), channel_id=1, source_target_pairs={{0,8},{8,0},{16,24},{24,16},{32,40},{40,32},{48,56},{56,48},{64,72... | collective-permute-start | bytes 73736 | tf_op jit(solution)/shard_map/ppermute | solution.py:267
  16.1 0.8 collective-permute-done
  17.0 21.2 %all_gather.10 = bf16[8,2,32,384]{3,2,1,0:T(8,128)(2,1)} all-gather(bf16[1,2,32,384]{3,2,1,0:T(8,128)(2,1)S(1)} %maximum_select_fusion), channel_id=1, replica_groups=mesh['ctx'=64,'head'=8] {'head'}, dimensions={0}, use_global_device_ids=true | all-gather | bytes 442368 | tf_op jit(solution)/shard_map/all_gather | solution.py:270
  38.2 0.0 all-gather.3.cloned.1.call-update
  38.2 0.0 copy-start
  38.2 1.4 copy-done
  39.6 0.0 copy-start.1
  39.6 1.0 copy-done.1
  40.6 80.8 %attention.1 = bf16[2,128,3072]{2,1,0:T(8,128)(2,1)S(1)} custom-call(bf16[128,6144]{1,0:T(8,128)(2,1)S(1)} %bitcast.33, bf16[128,2048]{1,0:T(8,128)(2,1)S(1)} %bitcast.34), custom_call_target="tpu_custom_call" | custom-call | flops 2000000000 | bytes 200000000 | tf_op jit(solution)/shard_map/attention/pallas_call | solution.py:239
  121.4 49.0 %all-gather.3.cloned.1.call-done = bf16[256,2,32,384]{3,2,1,0:T(8,128)(2,1)} async-done(((bf16[8,2,32,384]{3,2,1,0:T(8,128)(2,1)}), bf16[256,2,32,384]{3,2,1,0:T(8,128)(2,1)}) %all-gather.3.cloned.1.call-update) | async-done | bytes 12582928 | tf_op jit(solution)/shard_map/all_gather | solution.py:271
  170.4 11.6 %copy.7 = bf16[32,2,32,384,8]{3,2,1,0,4:T(8,128)(2,1)} copy(bf16[32,2,32,384,8]{3,2,1,4,0:T(8,128)(2,1)} %bitcast.36) | data formatting | bytes 25165824 | tf_op jit(solution)/shard_map/btyf,xyprf->btxpr/dot_general | solution.py:274
  182.0 6.4 %convolution_bitcast_fusion = f32[2,128,2048]{2,1,0:T(8,128)S(1)} fusion(bf16[2048,384,8,1]{1,0,2,3:T(8,128)(2,1)} %bitcast.37, bf16[2,16,8,8,384]{4,3,2,1,0:T(8,128)(2,1)S(1)} %bitcast.35), kind=kOutput, calls=%fused_computation | convolution fusion | flops 3221225472 | bytes 16252928 | tf_op jit(solution)/shard_map/btyf,xyprf->btxpr/dot_general | solution.py:274
  188.5 0.1 fusion.3
  188.6 3.0 %collective-permute-start.1 = (bf16[128,2048]{1,0:T(8,128)(2,1)S(1)}, bf16[128,2048]{1,0:T(8,128)(2,1)S(1)}, u32[]{:S(2)}, u32[]{:S(2)}) collective-permute-start(bf16[128,2048]{1,0:T(8,128)(2,1)S(1)} %fusion.3), channel_id=1, source_target_pairs={{0,8},{8,0},{16,24},{24,16},{32,40},{40,32},{48,56},{56,48},{64,72... | collective-permute-start | bytes 1572872 | tf_op jit(solution)/shard_map/ppermute | solution.py:278
  191.5 1.5 collective-permute-done.1
  193.0 1.1 fusion.2
  (2 shorter events, 0.0 us)
Async XLA Ops:
  6.5 163.9 %all-gather.3.cloned.1.call-start = ((), (), s32[]{:S(2)}) async-start(), calls=%async_computation | async-start | bytes 12976128 | tf_op jit(solution)/shard_map/all_gather | solution.py:271
  7.3 9.6 %collective-permute-start = (bf16[32,384]{1,0:T(8,128)(2,1)S(1)}, bf16[32,384]{1,0:T(8,128)(2,1)S(1)}, u32[]{:S(2)}, u32[]{:S(2)}) collective-permute-start(bf16[32,384]{1,0:T(8,128)(2,1)S(1)} %get-tuple-element.6), channel_id=1, source_target_pairs={{0,8},{8,0},{16,24},{24,16},{32,40},{40,32},{48,56},{56,48},{64,72... | collective-permute-start | bytes 73736 | tf_op jit(solution)/shard_map/ppermute | solution.py:267
  38.2 1.4 copy-start
  39.6 1.0 copy-start.1
  188.6 4.5 %collective-permute-start.1 = (bf16[128,2048]{1,0:T(8,128)(2,1)S(1)}, bf16[128,2048]{1,0:T(8,128)(2,1)S(1)}, u32[]{:S(2)}, u32[]{:S(2)}) collective-permute-start(bf16[128,2048]{1,0:T(8,128)(2,1)S(1)} %fusion.3), channel_id=1, source_target_pairs={{0,8},{8,0},{16,24},{24,16},{32,40},{40,32},{48,56},{56,48},{64,72... | collective-permute-start | bytes 1572872 | tf_op jit(solution)/shard_map/ppermute | solution.py:278
Sparse Core Ops, SparseCore 0:
  38.3 132.0 all-gather.2

commit v2 on v1

--- a/solution.py
+++ b/solution.py
@@ -13,6 +13,17 @@
 MESH = pl.DeviceIdType.MESH
 NX, NY, NZ = 4, 8, 8
 F32, BF16 = jnp.float32, jnp.bfloat16
+TILE = 256
+PLAN = [
+    [("a", 0), ("b", 0)],
+    [],
+    [],
+    [("a", 1)],
+    [("a", 2), ("b", 1)],
+    [("a", 3), ("b", 2)],
+    [("a", 4), ("b", 3), ("a", 5), ("b", 4), ("a", 6)],
+    [("a", 7), ("b", 5), ("a", 8), ("b", 6)],
+]
 
 
 def where_am_i():
@@ -41,10 +52,11 @@
     return pl.ds(pl.multiple_of(index * width, width), width)
 
 
-def attention_kernel(
-    factor, qkv_ref, grad_ref, out_ref,
-    got_qkv, got_grad, states, arrived, before, intra, total, z_in, x_in, z_out, base,
+def layer_kernel(
+    factor, qkv_ref, grad_ref, w_ref, out_ref,
+    got_qkv, got_grad, states, arrived, before, intra, total, z_in, x_in, z_out, base, grads, weight, give, take,
     core_sem, state_send, state_recv, z_send, z_recv, x_send, x_recv, b_send, b_recv, p_send, p_recv,
+    w_sem, first_sem, ring_sem, line_sem, cross_sem, long_sem, tile_sem,
 ):
     x, y, z, c = where_am_i()
     other = 1 - c
@@ -59,6 +71,112 @@
     for peer in everyone:
         pl.semaphore_signal(barrier, inc=1, device_id=peer, device_id_type=MESH)
     pl.semaphore_wait(barrier, len(everyone))
+
+    spot = x * NZ + z
+    rows = w_ref.shape[0]
+    half = rows // 2
+
+    def send(ref, sems, at, peer):
+        return pltpu.make_async_remote_copy(
+            ref, ref, sems.at[(0,) + at], sems.at[(1,) + at], device_id=peer, device_id_type=MESH)
+
+    own_half = pl.ds(pl.multiple_of(c * rows, rows), rows)
+    swap_w = pltpu.make_async_remote_copy(
+        w_ref.at[:, lanes(other, W3)], weight.at[y, spot, own_half],
+        w_sem.at[0], w_sem.at[1], device_id=partner, device_id_type=MESH)
+    swap_w.start()
+
+    def side(way, last):
+        return pl.ds(0 if way > 0 else half, half) if last else pl.ds(0, rows)
+
+    def side_z(way, last):
+        return pl.ds(rows if way > 0 else rows + half, half) if last else pl.ds(rows, rows)
+
+    def way_at(way):
+        return 0 if way > 0 else 1
+
+    def a_first(k):
+        return send(weight.at[y, spot, pl.ds(0, rows)], first_sem, (0, k), ring_z(k))
+
+    def b_first(k):
+        return send(weight.at[y, spot, pl.ds(rows, rows)], first_sem, (1, k), ring_y(k))
+
+    def a_ring(way, d):
+        block = weight.at[lax.rem(y - way * d + NY, NY), pl.ds(x * NZ, NZ), side(way, d == NY // 2 - 1)]
+        return send(block, ring_sem, (way_at(way), d), ring_y(way % NY))
+
+    order = [0, -1, 1, -2, 2, -3, 3, 4]
+
+    def a_line(t, way, d):
+        at = lax.rem(x - way * d + NX, NX)
+        block = weight.at[lax.rem(y + order[t] + NY, NY), pl.ds(at * NZ, NZ), side(way, d == 1)]
+        return send(block, line_sem, (t, way_at(way), d), ring_x(way % NX))
+
+    def b_cross(way, d):
+        at = lax.rem(x - way * d + NX, NX)
+        return send(weight.at[:, at * NZ + z, side_z(way, d == 1)], cross_sem, (way_at(way), d), ring_x(way % NX))
+
+    def b_long(b, way, d):
+        at = lax.rem(x + (0, -1, 1, 2)[b] + NX, NX) * NZ + lax.rem(z - way * d + NZ, NZ)
+        block = weight.at[:, at, side_z(way, d == NZ // 2 - 1)]
+        return send(block, long_sem, (b, way_at(way), d), ring_z(way % NZ))
+
+    both = (1, -1)
+
+    def step_a(t):
+        if t == 0:
+            for way in both:
+                a_ring(way, 0).start()
+        elif t < NY - 1:
+            way, d = both[(t - 1) % 2], (t - 1) // 2
+            a_ring(way, d).wait_recv()
+            a_ring(way, d + 1).start()
+        elif t == NY - 1:
+            for way in both:
+                a_ring(way, NY // 2 - 1).wait_recv()
+        if t < NY:
+            for way in both:
+                a_line(t, way, 0).start()
+        if t >= 1:
+            for way in both:
+                a_line(t - 1, way, 0).wait_recv()
+                a_line(t - 1, way, 1).start()
+
+    def step_b(s):
+        if s == 0:
+            for way in both:
+                b_cross(way, 0).start()
+        elif s == 1:
+            for way in both:
+                b_cross(way, 0).wait_recv()
+                b_cross(way, 1).start()
+        elif s == 3:
+            for way in both:
+                b_cross(way, 1).wait_recv()
+        if s < NX:
+            for way in both:
+                b_long(s, way, 0).start()
+        for d in range(NZ // 2 - 1):
+            b = s - 1 - d
+            if 0 <= b < NX:
+                for way in both:
+                    b_long(b, way, d).wait_recv()
+                    b_long(b, way, d + 1).start()
+
+    def finish_weight():
+        for way in both:
+            for t in range(NY):
+                a_line(t, way, 1).wait_recv()
+                a_line(t, way, 0).wait_send()
+                a_line(t, way, 1).wait_send()
+            for d in range(NY // 2):
+                a_ring(way, d).wait_send()
+            for d in range(2):
+                b_cross(way, d).wait_send()
+            for b in range(NX):
+                b_long(b, way, NZ // 2 - 1).wait_recv()
+                for d in range(NZ // 2):
+                    b_long(b, way, d).wait_send()
 
     def swap(j):
         send = pltpu.make_async_remote_copy(
@@ -79,6 +197,35 @@
 
     lax.fori_loop(0, NY, start_swap, 0)
 
+    weight[y, spot, own_half, :] = w_ref[:, lanes(c, W3)]
+    swap_w.wait()
+
+    def start_first(k, carry):
+        a_first(k).start()
+        b_first(k).start()
+        return carry
+
+    lax.fori_loop(1, NY, start_first, 0)
+
+    def wait_a_first(k, carry):
+        a_first(k).wait()
+        return carry
+
+    def wait_b_first(k, carry):
+        b_first(k).wait()
+        return carry
+
+    def run(steps):
+        for name, number in steps:
+            if name == "a":
+                if number == 0:
+                    lax.fori_loop(1, NZ, wait_a_first, 0)
+                step_a(number)
+            else:
+                if number == 0:
+                    lax.fori_loop(1, NY, wait_b_first, 0)
+                step_b(number)
+
     def own_rows(j):
         at = (2 * j + c) * W3
         part = lambda i: qkv_ref[:, pl.ds(pl.multiple_of(at + i * DH, DH), DH)]
@@ -107,10 +254,13 @@
         state_copy(k).start()
         return carry
 
-    lax.fori_loop(1, NY, make_states, 0)
+    lax.fori_loop(1, 5, make_states, 0)
+    run(PLAN[0])
+    lax.fori_loop(5, NY, make_states, 0)
     for copy in swap(y):
         copy.wait()
     block_states(arrived, y)
+    run(PLAN[1])
 
     rows_at = lax.broadcasted_iota(jnp.int32, (DH, DH), 0)
     cols_at = lax.broadcasted_iota(jnp.int32, (DH, DH), 1)
@@ -126,7 +276,9 @@
             intra[slot, j, 2] = tn(qk, g)
         return carry
 
-    lax.fori_loop(0, NY, inside, 0)
+    for piece in range(4):
+        lax.fori_loop(2 * piece, 2 * piece + 2, inside, 0)
+        run(PLAN[2 + piece])
 
     def wait_state(k, carry):
         state_copy(k).wait()
@@ -209,18 +361,19 @@
         return carry
 
     lax.fori_loop(1, NY, start_p, 0)
+    run(PLAN[6])
     for slot in range(2):
         for kind in range(2):
             before[y, slot, kind] = states[y, slot, kind]
 
     def finish(j):
-        for slot, rows in ((c, own_rows(j)), (other, got_rows(j))):
-            q, k, v, g = rows
+        for slot, mine, rows_of in ((c, 0, own_rows), (other, 1, got_rows)):
+            q, k, v, g = rows_of(j)
             kv, qg = before[j, slot, 0], before[j, slot, 1]
             at = lambda i: pl.ds(pl.multiple_of(j * W3 + i * DH, DH), DH)
-            out_ref[slot, :, at(0)] = ((intra[slot, j, 0] + nt(g, kv)) * factor).astype(BF16)
-            out_ref[slot, :, at(1)] = ((intra[slot, j, 1] + nt(v, qg)) * factor).astype(BF16)
-            out_ref[slot, :, at(2)] = ((intra[slot, j, 2] + nn(k, qg)) * factor).astype(BF16)
+            grads[mine, :, at(0)] = ((intra[slot, j, 0] + nt(g, kv)) * factor).astype(BF16)
+            grads[mine, :, at(1)] = ((intra[slot, j, 1] + nt(v, qg)) * factor).astype(BF16)
+            grads[mine, :, at(2)] = ((intra[slot, j, 2] + nn(k, qg)) * factor).astype(BF16)
 
     finish(y)
 
@@ -230,17 +383,51 @@
         return carry
 
     lax.fori_loop(1, NY, finish_got, 0)
-
-
-def attention(qkv, grad, factor):
+    run(PLAN[7])
+    finish_weight()
+
+    tiles = NX * NZ * 2 * rows // TILE
+    spots = TILE // (2 * rows)
+
+    def tile_copy(i):
+        return pltpu.make_async_remote_copy(
+            give.at[:, lanes(i, TILE)], take.at[:, lanes(i, TILE)],
+            tile_sem.at[0, i], tile_sem.at[1, i], device_id=partner, device_id_type=MESH)
+
+    def project(i, carry):
+        acc = jnp.zeros((2 * DH, TILE), F32)
+        for j in range(NY):
+            left = grads[:, :, j * W3:(j + 1) * W3].reshape(2 * DH, W3)
+            right = weight[j, pl.ds(i * spots, spots)].reshape(TILE, W3)
+            acc = acc + nt(left, right)
+        give[:, lanes(i, TILE)] = acc[DH:].astype(BF16)
+        tile_copy(i).start()
+        out_ref[:, lanes(i, TILE)] = acc[:DH]
+        return carry
+
+    lax.fori_loop(0, tiles, project, 0)
+
+    def add_partner(i, carry):
+        tile_copy(i).wait()
+        out_ref[:, lanes(i, TILE)] += take[:, lanes(i, TILE)].astype(F32)
+        return carry
+
+    lax.fori_loop(0, tiles, add_partner, 0)
+
+
+def layer(qkv, grad, w, factor):
     state = pltpu.VMEM((NY, 2, 2, DH, DH), BF16)
     part = 2 * DH // NZ
-    pairs = [pltpu.SemaphoreType.DMA((n,)) for n in (NY, NY, NZ, NZ, NX, NX, NZ, NZ, NY, NY)]
+    rows = w.shape[0]
+    width = NX * NZ * 2 * rows
+    dma = pltpu.SemaphoreType.DMA
+    pairs = [dma((n,)) for n in (NY, NY, NZ, NZ, NX, NX, NZ, NZ, NY, NY)]
+    vmem = pl.BlockSpec(memory_space=pltpu.VMEM)
     return pl.pallas_call(
-        functools.partial(attention_kernel, factor),
-        out_shape=jax.ShapeDtypeStruct((2, DH, NY * W3), BF16),
-        in_specs=[pl.BlockSpec(memory_space=pltpu.VMEM)] * 2,
-        out_specs=pl.BlockSpec(memory_space=pltpu.VMEM),
+        functools.partial(layer_kernel, factor),
+        out_shape=jax.ShapeDtypeStruct((DH, width), F32),
+        in_specs=[vmem] * 3,
+        out_specs=vmem,
         scratch_shapes=[
             pltpu.VMEM((DH, NY * W3), BF16), pltpu.VMEM((DH, NY * DH), BF16),
             state, state, state,
@@ -248,35 +435,22 @@
             pltpu.VMEM((2 * DH, DH), F32), pltpu.VMEM((NZ, part, DH), F32),
             pltpu.VMEM((NX, part, DH), F32), pltpu.VMEM((NZ, part, DH), F32),
             pltpu.VMEM((2 * DH, DH), F32),
-            pltpu.SemaphoreType.DMA((4, NY)), *pairs,
+            pltpu.VMEM((2, DH, NY * W3), BF16),
+            pltpu.VMEM((NY, NX * NZ, 2 * rows, W3), BF16),
+            pltpu.VMEM((DH, width), BF16), pltpu.VMEM((DH, width), BF16),
+            dma((4, NY)), *pairs,
+            dma((2,)), dma((2, 2, NY)), dma((2, 2, NY // 2)), dma((2, NY, 2, 2)), dma((2, 2, 2)),
+            dma((2, NX, 2, NZ // 2)), dma((2, width // TILE)),
         ],
         compiler_params=pltpu.CompilerParams(
-            collective_id=0, has_side_effects=True, vmem_limit_bytes=24 << 20),
-        cost_estimate=pl.CostEstimate(flops=2 * 10**9, bytes_accessed=200 * 10**6, transcendentals=0),
-        name="attention",
-    )(qkv, grad)
+            collective_id=0, has_side_effects=True, vmem_limit_bytes=44 << 20),
+        name="layer",
+    )(qkv, grad, w)
 
 
 def per_device(qkv, grad_out, w_qkv):
-    n = lax.axis_size("ctx")
-    factor = 1.0 / math.sqrt(DH * DH * NY * n)
-    c = lax.rem(lax.axis_index("ctx"), 2)
-    halves = jnp.stack([w_qkv[:, :W3], w_qkv[:, W3:]])
-    keep = lax.dynamic_index_in_dim(halves, c, 0, False)
-    give = lax.dynamic_index_in_dim(halves, 1 - c, 0, False)
-    got = lax.ppermute(give, "ctx", [(i, i ^ 1) for i in range(n)])
-    pair = jnp.where(c == 0, jnp.stack([keep, got]), jnp.stack([got, keep]))
-    groups = [[2 * i + core for i in range(n // 2)] for core in range(2)]
-    by_head = lax.all_gather(pair, "head")
-    whole = lax.all_gather(by_head, "ctx", axis_index_groups=groups)
-    grads = attention(qkv[0], grad_out[0], factor)
-    grads = grads.reshape(2, DH, NY, W3)
-    partial = jnp.einsum("btyf,xyprf->btxpr", grads, whole, preferred_element_type=F32)
-    partial = partial.reshape(2, DH, -1)
-    mine = lax.dynamic_index_in_dim(partial, c, 0, False)
-    theirs = lax.dynamic_index_in_dim(partial, 1 - c, 0, False).astype(BF16)
-    other = lax.ppermute(theirs, "ctx", [(i, i ^ 1) for i in range(n)])
-    return (mine + other.astype(F32))[None]
+    factor = 1.0 / math.sqrt(DH * DH * NY * lax.axis_size("ctx"))
+    return layer(qkv[0], grad_out[0], w_qkv, factor)[None]
 
 
 def solution(mesh):

time: 201 us -> 147 us (0.73)
  Pallas kernels: 80.8 us -> 141 us
  waiting for transfers between devices: 51.3 us -> 0 us
  blocking collectives: 21.2 us -> 0 us
  between operations: 13.5 us -> 0.01 us
  starting transfers between devices: 11.7 us -> 0 us
  local copies, waits for them, and re-layouts: 14.9 us -> 4.22 us
  matrix products: 6.45 us -> 0 us
    pallas_call x1, Pallas kernels: 80.8 us -> 141 us  [layer(): pl.pallas_call(functools.partial(layer_kernel, factor), out_shape=jax.Sha...]
    all_gather x1 -> x0, waiting for transfers between devices: 49 us -> none  [per_device(): whole = lax.all_gather(by_head, 'ctx', axis_index_groups=groups)]
    all_gather x1 -> x0, blocking collectives: 21.2 us -> none  [per_device(): by_head = lax.all_gather(pair, 'head')]
    ppermute x2 -> x0, starting transfers between devices: 11.7 us -> none  [the longest x1 8.79 us: per_device(): got = lax.ppermute(give, 'ctx', [(i, i ^ 1) for i in range(n)])]
    dot_general x1 -> x0, local copies, waits for them, and re-layouts: 11.6 us -> none  [per_device(): jnp.einsum('btyf,xyprf->btxpr', grads, whole, preferred_element_type=F32)]
    dot_general x1 -> x0, matrix products: 6.45 us -> none  [per_device(): jnp.einsum('btyf,xyprf->btxpr', grads, whole, preferred_element_type=F32)]
    ppermute x2 -> x0, waiting for transfers between devices: 2.34 us -> none  [the longest x1 1.51 us: per_device(): other = lax.ppermute(theirs, 'ctx', [(i, i ^ 1) for i in range(n)])]
    unnamed x4 -> x7, local copies, waits for them, and re-layouts: 2.44 us -> 4.22 us
  transfers between devices with their start and end apart: 3 -> 0, of which waited for: 3 -> 0; matrix products, arithmetic and copies ran while one was open for 0% -> 0% of each run, Pallas kernels for 40% -> 0%
where the time goes in v2:
time: 147 us; the launch traced here: 145 us
  Pallas kernels  141 us (96%)
  local copies, waits for them, and re-layouts  4.22 us (3%)
    pallas_call x1, Pallas kernels, layer(): pl.pallas_call(functools.partial(layer_kernel, factor), out_shape=jax.Sha...  141 us
    unnamed x7, local copies, waits for them, and re-layouts  4.22 us

profile of v2, /device:TPU:1, one launch (start us, length us, event | category | flops | bytes accessed | tf_op | source)
XLA Modules:
  0.0 145.4 jit_solution(442424038963758051)
XLA Ops:
  0.0 0.0 copy-start
  0.0 1.4 copy-done
  1.4 0.0 copy-start.1
  1.4 1.0 copy-done.1
  2.5 0.0 copy-start.2
  2.5 0.8 copy-done.2
  3.2 141.2 %layer.1 = f32[128,2048]{1,0:T(8,128)S(1)} custom-call(bf16[128,6144]{1,0:T(8,128)(2,1)S(1)} %bitcast.4, bf16[128,2048]{1,0:T(8,128)(2,1)S(1)} %bitcast.5, bf16[32,768]{1,0:T(8,128)(2,1)S(1)} %copy-done.2), custom_call_target="tpu_custom_call" | custom-call | tf_op jit(solution)/shard_map/layer/pallas_call | solution.py:426
  144.4 1.0 copy.5
Async XLA Ops:
  0.0 1.4 copy-start
  1.4 1.0 copy-start.1
  2.5 0.8 copy-start.2

commit v3 on v0

v3 whole, which is shorter than its diff:
```python
import functools
import math

import jax
import jax.numpy as jnp
from jax import lax
from jax.experimental import pallas as pl
from jax.experimental.pallas import tpu as pltpu
from jax.sharding import PartitionSpec as P

DH = 128
W3 = 3 * DH
MESH = pl.DeviceIdType.MESH
NX, NY, NZ = 4, 8, 8
F32, BF16 = jnp.float32, jnp.bfloat16
TILE = 256
ORDER = [
    "m0", "S0", "l0", "m1", "i0", "Z00", "C1", "R1", "L0", "i1", "t0", "Z01", "z0", "L1", "C2", "R2",
    "x0", "Z10", "Z20", "L2", "b0", "t1", "Z02", "R3", "z1", "Z11", "L3", "x1", "Z21", "L4", "b1", "Z30",
    "R4", "i2", "i3", "Z12", "L5", "f0", "Z22", "L6", "Z31", "L7", "f1", "Z32",
]


def where_am_i():
    ctx, y = lax.axis_index("ctx"), lax.axis_index("head")
    c, xz = lax.rem(ctx, 2), lax.div(ctx, 2)
    return lax.div(xz, NZ), y, lax.rem(xz, NZ), c


def device(x, y, z, c):
    return ((x * NZ + z) * 2 + c, y)


def nn(a, b):
    return lax.dot_general(a, b, (((1,), (0,)), ((), ())), preferred_element_type=F32)


def nt(a, b):
    return lax.dot_general(a, b, (((1,), (1,)), ((), ())), preferred_element_type=F32)


def tn(a, b):
    return lax.dot_general(a, b, (((0,), (0,)), ((), ())), preferred_element_type=F32)


def lanes(index, width):
    return pl.ds(pl.multiple_of(index * width, width), width)


def layer_kernel(
    factor, qkv_hbm, grad_hbm, w_hbm, out_ref,
    qkv_ref, grad_ref, w_ref, got_qkv, got_grad, states, arrived, before, intra,
    total, z_in, x_in, z_out, base, grads, weight, give, take,
    load_sem, core_sem, state_sem, z_sem, x_sem, b_sem, p_sem,
    first_sem, got_sem, ring_sem, line_sem, cross_sem, long_sem, tile_sem,
):
    x, y, z, c = where_am_i()
    other = 1 - c
    ring_y = lambda k: device(x, lax.rem(y + k, NY), z, c)
    ring_z = lambda k: device(x, y, lax.rem(z + k, NZ), c)
    ring_x = lambda k: device(lax.rem(x + k, NX), y, z, c)
    partner = device(x, y, z, other)

    loads = [
        pltpu.make_async_copy(w_hbm, w_ref, load_sem.at[0]),
        pltpu.make_async_copy(qkv_hbm, qkv_ref, load_sem.at[1]),
        pltpu.make_async_copy(grad_hbm, grad_ref, load_sem.at[2]),
    ]
    for load in loads:
        load.start()

    barrier = pltpu.get_barrier_semaphore()
    everyone = [partner] + [ring_y(k) for k in range(1, NY)]
    everyone += [ring_z(k) for k in range(1, NZ)] + [ring_x(k) for k in range(1, NX)]
    everyone += [device(x, lax.rem(y + k * other, NY), lax.rem(z + k * c, NZ), other) for k in range(1, NZ)]
    for peer in everyone:
        pl.semaphore_signal(barrier, inc=1, device_id=peer, device_id_type=MESH)
    pl.semaphore_wait(barrier, len(everyone))

    def remote(src, dst, sems, at, peer):
        return pltpu.make_async_remote_copy(
            src, dst, sems.at[(0,) + at], sems.at[(1,) + at], device_id=peer, device_id_type=MESH)

    def y_of(k):
        return lax.rem(y + k, NY)

    def loop(first, last, do):
        def one(k, carry):
            do(k)
            return carry

        lax.fori_loop(first, last, one, 0)

    spot = x * NZ + z
    rows = w_ref.shape[0]
    half = rows // 2
    own_half = pl.ds(pl.multiple_of(c * rows, rows), rows)

    def first_to(core, k):
        peer = device(x, lax.rem(y + k * c, NY), lax.rem(z + k * other, NZ), core)
        return pltpu.make_async_remote_copy(
            w_hbm.at[:, lanes(core, W3)], weight.at[y, spot, own_half],
            first_sem.at[core, k], got_sem.at[c, k], device_id=peer, device_id_type=MESH)

    def first_from(row, k):
        block = weight.at[y, spot, pl.ds(row * rows, rows)]
        return pltpu.make_async_remote_copy(
            block, block, first_sem.at[row, k], got_sem.at[row, k], device_id=partner, device_id_type=MESH)

    first_to(other, 0).start()

    def start_first(k):
        for core in range(2):
            first_to(core, k).start()

    loop(1, NY, start_first)

    def swap(j):
        return remote(qkv_hbm.at[:, lanes(2 * j + other, W3)], got_qkv.at[:, lanes(j, W3)], core_sem, (0, j), partner)

    def swap_grad(j):
        return remote(grad_hbm.at[:, lanes(2 * j + other, DH)], got_grad.at[:, lanes(j, DH)], core_sem, (1, j), partner)

    loop(1, NY + 1, lambda k: swap(y_of(k)).start())
    loop(1, NY + 1, lambda k: swap_grad(y_of(k)).start())

    def side(way, last):
        return pl.ds(0 if way > 0 else half, half) if last else pl.ds(0, rows)

    def side_z(way, last):
        return pl.ds(rows if way > 0 else rows + half, half) if last else pl.ds(rows, rows)

    def way_at(way):
        return 0 if way > 0 else 1

    def same(ref, sems, at, peer):
        return remote(ref, ref, sems, at, peer)

    def a_ring(way, d):
        block = weight.at[lax.rem(y - way * d + NY, NY), pl.ds(x * NZ, NZ), side(way, d == NY // 2 - 1)]
        return same(block, ring_sem, (way_at(way), d), ring_y(way % NY))

    order = [0, -1, 1, -2, 2, -3, 3, 4]

    def a_line(t, way, d):
        at = lax.rem(x - way * d + NX, NX)
        block = weight.at[lax.rem(y + order[t] + NY, NY), pl.ds(at * NZ, NZ), side(way, d == 1)]
        return same(block, line_sem, (t, way_at(way), d), ring_x(way % NX))

    def b_cross(way, d):
        at = lax.rem(x - way * d + NX, NX)
        return same(weight.at[:, at * NZ + z, side_z(way, d == 1)], cross_sem, (way_at(way), d), ring_x(way % NX))

    near = [0, -1, 1, 2]

    def b_long(b, way, d):
        at = lax.rem(x + near[b] + NX, NX) * NZ + lax.rem(z - way * d + NZ, NZ)
        block = weight.at[:, at, side_z(way, d == NZ // 2 - 1)]
        return same(block, long_sem, (b, way_at(way), d), ring_z(way % NZ))

    both = (1, -1)

    def set_off():
        loop(c, NY, lambda k: first_from(1, k).wait_recv())
        for way in both:
            b_cross(way, 0).start()
        for way in both:
            b_long(0, way, 0).start()
        loop(other, NZ, lambda k: first_from(0, k).wait_recv())
        for way in both:
            a_ring(way, 0).start()

    def start_line():
        for way in both:
            a_line(0, way, 0).start()

    def pass_ring(i):
        for n, way in enumerate(both):
            a_ring(way, i - 1).wait_recv()
            if i < NY // 2:
                a_ring(way, i).start()
                for on in both:
                    a_line(2 * i - 1 + n, on, 0).start()
        if i == NY // 2:
            for on in both:
                a_line(NY - 1, on, 0).start()

    def pass_cross(i):
        for way in both:
            b_cross(way, i - 1).wait_recv()
            if i == 1:
                b_cross(way, 1).start()
        for b in ((1, 2), (3,))[i - 1]:
            for way in both:
                b_long(b, way, 0).start()

    def pass_long(b, d):
        for way in both:
            b_long(b, way, d).wait_recv()
            b_long(b, way, d + 1).start()

    def pass_line(t):
        for way in both:
            a_line(t, way, 0).wait_recv()
            a_line(t, way, 1).start()

    loads[0].wait()
    weight[y, spot, own_half, :] = w_ref[:, lanes(c, W3)]

    def own_rows(j):
        at = (2 * j + c) * W3
        part = lambda i: qkv_ref[:, pl.ds(pl.multiple_of(at + i * DH, DH), DH)]
        return part(0), part(1), part(2), grad_ref[:, lanes(2 * j + c, DH)]

    def got_rows(j):
        part = lambda i: got_qkv[:, pl.ds(pl.multiple_of(j * W3 + i * DH, DH), DH)]
        return part(0), part(1), part(2), got_grad[:, lanes(j, DH)]

    sides = ((c, 0, own_rows), (other, 1, got_rows))

    def state_copy(kind, k):
        return remote(states.at[kind, y_of(k)], arrived.at[kind, y], state_sem, (kind, k), ring_y(k))

    def block_states(kind, into, j):
        for slot, _, rows_of in sides:
            q, k, v, g = rows_of(j)
            into[kind, j, slot] = (tn(q, g) if kind else tn(k, v)).astype(BF16)

    def make_states(kind):
        wait = swap_grad if kind else swap

        def one(k):
            wait(y_of(k)).wait()
            block_states(kind, states, y_of(k))
            state_copy(kind, k).start()

        loop(1, NY, one)
        wait(y).wait()
        block_states(kind, arrived, y)

    causal = lax.broadcasted_iota(jnp.int32, (DH, DH), 0) >= lax.broadcasted_iota(jnp.int32, (DH, DH), 1)

    def inside(j):
        for slot, _, rows_of in sides:
            q, k, v, g = rows_of(j)
            gv = jnp.where(causal, nt(g, v), 0.0).astype(BF16)
            qk = jnp.where(causal, nt(q, k), 0.0).astype(BF16)
            intra[slot, j, 0] = nn(gv, k)
            intra[slot, j, 1] = tn(gv, q)
            intra[slot, j, 2] = tn(qk, g)

    part = DH // NZ

    def slice_of(i):
        return pl.ds(pl.multiple_of(i * part, part), part)

    def z_copy(kind, k):
        return remote(total.at[kind, slice_of(lax.rem(z + k, NZ))], z_in.at[kind, z], z_sem, (kind, k), ring_z(k))

    def x_copy(kind, k):
        return remote(x_in.at[kind, x], x_in.at[kind, x], x_sem, (kind, k), ring_x(k))

    def b_copy(kind, k):
        return remote(z_out.at[kind, lax.rem(z + k, NZ)], base.at[kind, slice_of(z)], b_sem, (kind, k), ring_z(k))

    def p_copy(kind, k):
        return remote(states.at[kind, y_of(k)], before.at[kind, y], p_sem, (kind, k), ring_y(k))

    def scan_totals(kind):
        loop(1, NY, lambda k: state_copy(kind, k).wait())
        acc = jnp.zeros((DH, DH), F32)
        for j in range(NY):
            acc = acc + arrived[kind, j, 0].astype(F32) + arrived[kind, j, 1].astype(F32)
        total[kind] = acc
        for k in range(1, NZ):
            z_copy(kind, k).start()
        z_in[kind, z] = total[kind, slice_of(z), :]

    def scan_over_z(kind):
        for k in range(1, NZ):
            z_copy(kind, k).wait()
        acc = z_in[kind, 0]
        for i in range(1, NZ):
            acc = acc + z_in[kind, i]
        x_in[kind, x] = acc
        for k in range(1, NX):
            x_copy(kind, k).start()

    def scan_over_x(kind):
        for k in range(1, NX):
            x_copy(kind, k).wait()
        acc = jnp.zeros((part, DH), F32)
        for i in range(NX):
            acc = acc + jnp.where(i > x if kind else i < x, x_in[kind, i], 0.0)
        for i in reversed(range(NZ)) if kind else range(NZ):
            z_out[kind, i] = acc
            acc = acc + z_in[kind, i]
        for k in range(1, NZ):
            b_copy(kind, k).start()
        base[kind, slice_of(z), :] = z_out[kind, z]

    def scan_blocks(kind):
        for k in range(1, NZ):
            b_copy(kind, k).wait()
        acc = base[kind]
        for slot in (1, 0) if kind else (0, 1):
            for j in reversed(range(NY)) if kind else range(NY):
                states[kind, j, slot] = acc.astype(BF16)
                acc = acc + arrived[kind, j, slot].astype(F32)
        loop(1, NY, lambda k: p_copy(kind, k).start())
        for slot in range(2):
            before[kind, y, slot] = states[kind, y, slot]

    def finish(kind, j):
        for slot, mine, rows_of in sides:
            q, k, v, g = rows_of(j)
            state = before[kind, j, slot]
            at = lambda i: pl.ds(pl.multiple_of(j * W3 + i * DH, DH), DH)
            if kind == 0:
                grads[mine, :, at(0)] = ((intra[slot, j, 0] + nt(g, state)) * factor).astype(BF16)
            else:
                grads[mine, :, at(1)] = ((intra[slot, j, 1] + nt(v, state)) * factor).astype(BF16)
                grads[mine, :, at(2)] = ((intra[slot, j, 2] + nn(k, state)) * factor).astype(BF16)

    def finish_all(kind):
        finish(kind, y)

        def one(k):
            p_copy(kind, k).wait()
            finish(kind, lax.rem(y - k + NY, NY))

        loop(1, NY, one)

    def insides(first, last):
        loop(first, last, inside)

    tiles = NX * NZ * 2 * rows // TILE
    each = tiles // NX
    spots = TILE // (2 * rows)

    def tile_copy(i):
        return remote(give.at[:, lanes(i, TILE)], take.at[:, lanes(i, TILE)], tile_sem, (i,), partner)

    def project(i):
        acc = jnp.zeros((2 * DH, TILE), F32)
        for j in range(NY):
            left = grads[:, :, j * W3:(j + 1) * W3].reshape(2 * DH, W3)
            right = weight[j, pl.ds(i * spots, spots)].reshape(TILE, W3)
            acc = acc + nt(left, right)
        give[:, lanes(i, TILE)] = acc[DH:].astype(BF16)
        tile_copy(i).start()
        out_ref[:, lanes(i, TILE)] = acc[:DH]

    def project_x(b):
        at = lax.rem(x + near[b] + NX, NX) * each
        loop(at, at + each, project)

    def add_partner(i):
        tile_copy(i).wait()
        out_ref[:, lanes(i, TILE)] += take[:, lanes(i, TILE)].astype(F32)

    def load_and_make(kind):
        loads[1 + kind].wait()
        make_states(kind)

    acts = {
        "m": load_and_make, "t": scan_totals, "z": scan_over_z, "x": scan_over_x, "b": scan_blocks, "f": finish_all,
        "i": lambda n: insides(2 * n, 2 * n + 2), "S": lambda n: set_off(), "R": pass_ring, "C": pass_cross,
        "L": pass_line, "l": lambda n: start_line(), "Z": lambda n: pass_long(n // 10, n % 10),
    }
    for step in ORDER:
        acts[step[0]](int(step[1:]))

    last = NZ // 2 - 1
    for way in both:
        b_long(0, way, last).wait_recv()
    project_x(0)
    for b in (1, 2):
        for way in both:
            b_long(b, way, last).wait_recv()
        project_x(b)
    for way in both:
        b_long(3, way, last).wait_recv()
        for t in range(NY):
            a_line(t, way, 1).wait_recv()
    project_x(3)
    loop(0, tiles, add_partner)
    first_to(other, 0).wait_send()

    def wait_first(k):
        for core in range(2):
            first_to(core, k).wait_send()

    loop(1, NY, wait_first)
    for way in both:
        for d in range(2):
            b_cross(way, d).wait_send()
            for t in range(NY):
                a_line(t, way, d).wait_send()
        for d in range(NY // 2):
            a_ring(way, d).wait_send()
        for b in range(NX):
            for d in range(NZ // 2):
                b_long(b, way, d).wait_send()


def layer(qkv, grad, w, factor):
    part = DH // NZ
    rows = w.shape[0]
    width = NX * NZ * 2 * rows
    dma = pltpu.SemaphoreType.DMA
    state = pltpu.VMEM((2, NY, 2, DH, DH), BF16)
    return pl.pallas_call(
        functools.partial(layer_kernel, factor),
        out_shape=jax.ShapeDtypeStruct((DH, width), F32),
        in_specs=[pl.BlockSpec(memory_space=pltpu.HBM)] * 3,
        out_specs=pl.BlockSpec(memory_space=pltpu.VMEM),
        scratch_shapes=[
            pltpu.VMEM(qkv.shape, BF16), pltpu.VMEM(grad.shape, BF16), pltpu.VMEM(w.shape, BF16),
            pltpu.VMEM((DH, NY * W3), BF16), pltpu.VMEM((DH, NY * DH), BF16),
            state, state, state,
            pltpu.VMEM((2, NY, 3, DH, DH), F32),
            pltpu.VMEM((2, DH, DH), F32), pltpu.VMEM((2, NZ, part, DH), F32),
            pltpu.VMEM((2, NX, part, DH), F32), pltpu.VMEM((2, NZ, part, DH), F32),
            pltpu.VMEM((2, DH, DH), F32),
            pltpu.VMEM((2, DH, NY * W3), BF16),
            pltpu.VMEM((NY, NX * NZ, 2 * rows, W3), BF16),
            pltpu.VMEM((DH, width), BF16), pltpu.VMEM((DH, width), BF16),
            dma((3,)), dma((2, 2, NY)), dma((2, 2, NY)), dma((2, 2, NZ)), dma((2, 2, NX)),
            dma((2, 2, NZ)), dma((2, 2, NY)),
            dma((2, NY)), dma((2, NY)), dma((2, 2, NY // 2)), dma((2, NY, 2, 2)), dma((2, 2, 2)),
            dma((2, NX, 2, NZ // 2)), dma((2, width // TILE)),
        ],
        compiler_params=pltpu.CompilerParams(
            collective_id=0, has_side_effects=True, vmem_limit_bytes=60 << 20),
        name="layer",
    )(qkv, grad, w)


def per_device(qkv, grad_out, w_qkv):
    factor = 1.0 / math.sqrt(DH * DH * NY * lax.axis_size("ctx"))
    return layer(qkv[0], grad_out[0], w_qkv, factor)[None]


def solution(mesh):
    spec = P(None, ("ctx", "head"), None)
    return jax.shard_map(
        per_device, mesh=mesh, in_specs=(spec, spec, P("ctx", "head")), out_specs=spec, check_vma=False)
```

time: 460 us -> 110 us (0.24)
  waiting for transfers between devices: 259 us -> 0 us
  Pallas kernels: 0 us -> 107 us
  other arithmetic: 103 us -> 0 us
  matrix products: 37.1 us -> 0 us
  local copies, waits for them, and re-layouts: 28.3 us -> 2.3 us
  starting transfers between devices: 14.6 us -> 0 us
  between operations: 13.3 us -> 0.01 us
    all_gather x3 -> x0, waiting for transfers between devices: 170 us -> none  [the longest x2 88.1 us: carried_in(): gathered = lax.all_gather(x.astype(jnp.bfloat16), axis)]
    pallas_call x0 -> x1, Pallas kernels: none -> 107 us  [layer(): pl.pallas_call(functools.partial(layer_kernel, factor), out_shape=jax.Sha...]
    add x63 -> x0, other arithmetic: 54.4 us -> none  [combine_sum(): return earlier + later]
    reduce_scatter x1 -> x0, waiting for transfers between devices: 54.2 us -> none  [per_device(): lax.psum_scatter(jnp.einsum('stf,df->tsd', gradients, whole_weight, prefe...]
    unnamed x2 -> x0, other arithmetic: 45.8 us -> none
    dot_general x11 -> x0, matrix products: 37.1 us -> none  [the longest x1 7.98 us: per_device(): jnp.einsum('shtu,sthe->suhe', scores_qk, grad_wide, precision=highest)]
    all_to_all x2 -> x0, waiting for transfers between devices: 33.7 us -> none  [the longest x1 33.7 us: per_device(): lax.all_to_all(qkv, 'head', split_axis=2, concat_axis=1, tiled=True)]
    unnamed x17 -> x1, local copies, waits for them, and re-layouts: 22.1 us -> 2.3 us
  transfers between devices with their start and end apart: 6 -> 0, of which waited for: 5 -> 0; matrix products, arithmetic and copies ran while one was open for 29% -> 0% of each run, Pallas kernels for 0% -> 0%
where the time goes in v3:
time: 110 us
  Pallas kernels  107 us (97%)
  local copies, waits for them, and re-layouts  2.3 us (2%)
    pallas_call x1, Pallas kernels, layer(): pl.pallas_call(functools.partial(layer_kernel, factor), out_shape=jax.Sha...  107 us
    unnamed x1, local copies, waits for them, and re-layouts  2.3 us

profile of v3, /device:TPU:1, one launch (start us, length us, event | category | flops | bytes accessed | tf_op | source)
XLA Modules:
  0.0 109.6 jit_solution(3896238822183548228)
XLA Ops:
  0.0 107.3 %layer.1 = f32[128,2048]{1,0:T(8,128)} custom-call(bf16[128,6144]{1,0:T(8,128)(2,1)} %bitcast.4, bf16[128,2048]{1,0:T(8,128)(2,1)} %bitcast.5, bf16[32,768]{1,0:T(8,128)(2,1)} %w_hbm.1), custom_call_target="tpu_custom_call" | custom-call | tf_op jit(solution)/shard_map/layer/pallas_call | solution.py:413
  107.3 2.3 %copy.5 = f32[1,128,2048]{2,1,0:T(8,128)} copy(f32[1,128,2048]{2,1,0:T(8,128)} %bitcast.3) | data formatting | bytes 2097152

commit v4 on v3

--- a/solution.py
+++ b/solution.py
@@ -15,7 +15,7 @@
 F32, BF16 = jnp.float32, jnp.bfloat16
 TILE = 256
 ORDER = [
-    "m0", "S0", "l0", "m1", "i0", "Z00", "C1", "R1", "L0", "i1", "t0", "Z01", "z0", "L1", "C2", "R2",
+    "m0", "S0", "l0", "m1", "Z00", "C1", "R1", "L0", "i0", "i1", "t0", "Z01", "z0", "L1", "C2", "R2",
     "x0", "Z10", "Z20", "L2", "b0", "t1", "Z02", "R3", "z1", "Z11", "L3", "x1", "Z21", "L4", "b1", "Z30",
     "R4", "i2", "i3", "Z12", "L5", "f0", "Z22", "L6", "Z31", "L7", "f1", "Z32",
 ]

time: 110 us -> 110 us (level)
  no operation moved by 1% of the time
where the time goes in v4:
time: 110 us
  Pallas kernels  107 us (97%)
  local copies, waits for them, and re-layouts  2.3 us (2%)
    pallas_call x1, Pallas kernels, layer(): pl.pallas_call(functools.partial(layer_kernel, factor), out_shape=jax.Sha...  107 us
    unnamed x1, local copies, waits for them, and re-layouts  2.3 us

profile of v4, /device:TPU:1, one launch (start us, length us, event | category | flops | bytes accessed | tf_op | source)
XLA Modules:
  0.0 109.6 jit_solution(1821126669715090687)
XLA Ops:
  0.0 107.3 %layer.1 = f32[128,2048]{1,0:T(8,128)} custom-call(bf16[128,6144]{1,0:T(8,128)(2,1)} %bitcast.4, bf16[128,2048]{1,0:T(8,128)(2,1)} %bitcast.5, bf16[32,768]{1,0:T(8,128)(2,1)} %w_hbm.1), custom_call_target="tpu_custom_call" | custom-call | tf_op jit(solution)/shard_map/layer/pallas_call | solution.py:413
  107.3 2.3 %copy.5 = f32[1,128,2048]{2,1,0:T(8,128)} copy(f32[1,128,2048]{2,1,0:T(8,128)} %bitcast.3) | data formatting | bytes 2097152
